TPU v7x, 32 devices: a whole 2x2x4 slice. The times are simulated.
32 devices in a mesh: win: 2 (over y), row: 4 (over z), col: 4 (over x, core).
Axes of the slice: x: 2, y: 2, z: 4, core: 2. Of those that a mesh axis runs over, the one named last changes fastest.
Arguments:
- records: bfloat16 [32, 4096, 1024], P('win', ('row', 'col'))
- tile_pairs: int32 [4, 4, 4, 2], P('row', 'col'), may hold values from 0 to 3
- tile_count: int32 [4, 4], P('row', 'col'), may hold values from 1 to 4, as said below
- bin_index: int32 [32], replicated, may hold values from 1 to 511, as said below
Outputs:
- cross_tiles: bfloat16 [4, 4, 4, 2, 32, 256, 256], P('row', 'col', 'win')
Inputs may be any that keep to these rules, and one draw needn't show every extreme that they name: Slots 0 to tile_count - 1 of a cell are live; some cell has all 4 live and some cell one. `bin_index`: distinct and increasing; the first is 1 and the last 511.
All inputs are finite; a program needn't handle non-finite values.
Results may differ from a plain program's by a relative error of at most 0.0069.
Values may be sent and summed in bfloat16 or wider, within the bound.
A program may use at most 256 MiB of HBM per device.

v0:
```python
import math

import jax
import jax.numpy as jnp
from jax import lax
from jax.sharding import PartitionSpec as P


def dft_table(bin_index, length):
    sample_ids = jnp.arange(length, dtype=jnp.int32)
    phases = sample_ids[:, None] * bin_index[None, :] % length
    angles = 2.0 * math.pi / length * phases.astype(jnp.float32)
    window_taper = 0.5 - 0.5 * jnp.cos(2.0 * math.pi / length * sample_ids.astype(jnp.float32))
    cosine = window_taper[:, None] * jnp.cos(angles)
    sine = -window_taper[:, None] * jnp.sin(angles)
    return jnp.concatenate([cosine, sine], axis=1).astype(jnp.bfloat16)


def cross_spectra(first_block, second_block):
    second_real = second_block[:, 0]
    second_imag = second_block[:, 1]
    stacked = jnp.stack(
        [
            jnp.stack([second_real, second_imag], axis=1),
            jnp.stack([-second_imag, second_real], axis=1),
        ],
        axis=0,
    )
    return jnp.einsum(
        "wcktp,ewcktq->tekpq", first_block, stacked, preferred_element_type=jnp.float32
    )


def body(records, tile_pairs, tile_count, bin_index):
    length = records.shape[2]
    chan_block = records.shape[1]
    kept_bins = bin_index.shape[0]
    phase_table = dft_table(bin_index, length)
    spectrum = jnp.einsum("wcs,sk->wkc", records, phase_table, preferred_element_type=jnp.float32)
    energy = jnp.sqrt(jnp.mean(spectrum * spectrum, axis=1, keepdims=True) + 1e-06)
    whitened = (spectrum / energy).astype(jnp.bfloat16)
    whitened = lax.all_gather(whitened, "win", axis=0, tiled=True)
    row_set = lax.all_gather(whitened, "col", axis=2, tiled=True)
    column_set = lax.all_gather(whitened, "row", axis=2, tiled=True)
    window_rows = whitened.shape[0]
    row_blocks = row_set.reshape(window_rows, 2, kept_bins, lax.axis_size("col"), chan_block)
    column_blocks = column_set.reshape(window_rows, 2, kept_bins, lax.axis_size("row"), chan_block)
    slot_pairs = tile_pairs[0, 0]
    live_count = tile_count[0, 0]
    owned_slots = slot_pairs.shape[0] // lax.axis_size("win")
    begin_row = lax.axis_index("win") * owned_slots
    chosen = lax.dynamic_slice_in_dim(slot_pairs, begin_row, owned_slots, 0)
    positions = begin_row + jnp.arange(owned_slots, dtype=jnp.int32)
    first_chosen = jnp.take(row_blocks, chosen[:, 0], axis=3)
    second_chosen = jnp.take(column_blocks, chosen[:, 1], axis=3)
    live_mask = (positions < live_count).astype(jnp.float32)
    summed = cross_spectra(first_chosen, second_chosen) * live_mask[:, None, None, None, None]
    return summed.astype(jnp.bfloat16).reshape(
        1, 1, owned_slots, 2, kept_bins, chan_block, chan_block
    )


def solution(mesh):
    return jax.shard_map(
        body,
        mesh=mesh,
        in_specs=(
            P("win", ("row", "col"), None),
            P("row", "col", None, None),
            P("row", "col"),
            P(),
        ),
        out_specs=P("row", "col", "win", None, None, None, None),
        check_vma=False,
    )
```

profile of v0, /device:TPU:0, one launch (start us, length us, event | category | flops | bytes accessed | tf_op | source)
XLA Modules:
  0.0 217.1 jit_solution(18415207110802437952)
XLA Ops:
  6.5 0.0 copy-start
  6.5 0.0 all-gather.4.cloned.1.call-start
  6.6 1.3 multiply_convert_fusion.1
  7.8 6.1 %multiply_reduce_fusion = (f32[16,256]{1,0:T(8,128)S(1)}, f32[64,16,256]{2,0,1:T(8,128)S(1)}) fusion(bf16[16,256,1024]{2,1,0:T(8,128)(2,1)} %param.6, bf16[1024,32]{0,1:T(8,128)(2,1)S(1)} %get-tuple-element.13, bf16[1024,32]{0,1:T(8,128)(2,1)S(1)} %get-tuple-element.12), kind=kOutput, calls=%fused_computation.14 | convolution fusion | flops 537653248 | bytes 9584640 | tf_op jit(solution)/shard_map/wcs,sk->wkc/dot_general | solution.py:39
  13.9 0.9 fusion.8
  14.8 0.0 all-gather.4.cloned.1.call-update
  14.9 0.0 all-gather.6.cloned.1.call-start
  14.9 24.1 %all-gather.4.cloned.1.call-done = bf16[32,64,256]{2,1,0:T(8,128)(2,1)} async-done(((bf16[16,64,256]{2,1,0:T(8,128)(2,1)}), bf16[32,64,256]{2,1,0:T(8,128)(2,1)}) %all-gather.4.cloned.1.call-update) | async-done | bytes 1048592 | tf_op jit(solution)/shard_map/all_gather | solution.py:42
  39.0 0.0 all-gather.6.cloned.1.call-update
  39.0 0.0 all-gather.8.cloned.1.call-start
  39.1 0.7 all-gather.8.cloned.1.call-update
  40.4 0.0 copy-done
  40.4 0.1 constant_dynamic-slice_fusion
  40.5 0.1 copy.20
  40.6 0.2 slice_reduce_fusion
  40.9 80.3 %all-gather.6.cloned.1.call-done = bf16[32,64,1024]{2,1,0:T(8,128)(2,1)} async-done(((bf16[32,64,256]{2,1,0:T(8,128)(2,1)}), bf16[32,64,1024]{2,1,0:T(8,128)(2,1)}) %all-gather.6.cloned.1.call-update) | async-done | bytes 4194320 | tf_op jit(solution)/shard_map/all_gather | solution.py:44
  121.2 7.9 %reshape.42 = bf16[32,2,32,4,256]{4,3,2,1,0:T(4,128)(2,1)} reshape(bf16[32,64,1024]{2,1,0:T(8,128)(2,1)} %all-gather.6.cloned.1.call-done) | data formatting | bytes 8388608 | tf_op jit(solution)/shard_map/reshape | solution.py:47
  129.1 5.3 %copy.21 = bf16[32,2,32,4,256]{4,2,1,0,3:T(8,128)(2,1)} copy(bf16[32,2,32,4,256]{4,3,2,1,0:T(4,128)(2,1)} %reshape.42) | data formatting | bytes 8388608 | tf_op jit(solution)/shard_map/reshape | solution.py:47
  134.4 21.6 %all-gather.8.cloned.1.call-done = bf16[32,64,1024]{2,1,0:T(8,128)(2,1)} async-done(((bf16[32,64,256]{2,1,0:T(8,128)(2,1)}), bf16[32,64,1024]{2,1,0:T(8,128)(2,1)}) %all-gather.8.cloned.1.call-update) | async-done | bytes 4194320 | tf_op jit(solution)/shard_map/all_gather | solution.py:43
  156.0 7.8 %reshape.43 = bf16[32,2,32,4,256]{4,3,2,1,0:T(4,128)(2,1)} reshape(bf16[32,64,1024]{2,1,0:T(8,128)(2,1)} %all-gather.8.cloned.1.call-done) | data formatting | bytes 8388608 | tf_op jit(solution)/shard_map/reshape | solution.py:46
  163.8 4.9 %copy.24 = bf16[32,2,32,4,256]{4,2,1,0,3:T(8,128)(2,1)} copy(bf16[32,2,32,4,256]{4,3,2,1,0:T(4,128)(2,1)} %reshape.43) | data formatting | bytes 8388608 | tf_op jit(solution)/shard_map/reshape | solution.py:46
  168.8 2.9 %gather_fusion = bf16[2,32,2,32,256]{4,3,2,1,0:T(8,128)(2,1)S(1)} fusion(bf16[32,2,32,4,256]{4,2,1,0,3:T(8,128)(2,1)} %copy.21, s32[1024]{0:T(1024)S(1)} %pad_clamp_fusion.1), kind=kCustom, calls=%fused_computation.clone | custom fusion | bytes 4194312 | tf_op jit(solution)/shard_map/jit(_take)/gather | solution.py:55
  171.6 2.7 %fusion.6 = (bf16[1,32,2,32,2,256]{5,1,2,0,3,4:T(8,128)(2,1)}, bf16[32,2,32,2,256]{4,0,1,2,3:T(8,128)(2,1)S(1)}) fusion(bf16[2,32,2,32,256]{4,3,2,1,0:T(8,128)(2,1)S(1)} %gather_fusion, pred[2]{0:T(512)(128)(4,1)S(1)} %get-tuple-element.19), kind=kLoop, calls=%fused_computation.15 | loop fusion | flops 1048576 | bytes 6291458 | tf_op jit(solution)/shard_map/stack | solution.py:22
  174.3 1.1 slice_negate_fusion
  175.4 2.9 %gather_fusion.1 = bf16[2,32,2,32,256]{4,3,2,1,0:T(8,128)(2,1)S(1)} fusion(bf16[32,2,32,4,256]{4,2,1,0,3:T(8,128)(2,1)} %copy.24, s32[1024]{0:T(1024)S(1)} %pad_clamp_fusion), kind=kCustom, calls=%fused_computation.1.clone | custom fusion | bytes 4194312 | tf_op jit(solution)/shard_map/jit(_take)/gather | solution.py:54
  178.3 0.0 copy-start.2
  178.3 0.3 select_bitcast_fusion
  178.5 0.9 copy-done.2
  179.5 0.2 maximum_bitcast_fusion
  179.7 1.3 copy-done.3
  181.1 8.2 %fusion.1 = bf16[1,1,2,2,32,256,256]{5,6,3,4,2,1,0:T(8,128)(2,1)} fusion(f32[2]{0:T(128)S(1)} %compare_convert_fusion, bf16[1,32,2,32,2,256]{5,1,2,0,3,4:T(8,128)(2,1)S(1)} %maximum_bitcast_fusion, bf16[1,32,2,32,2,256]{5,1,2,0,3,4:T(8,128)(2,1)S(1)} %copy-done.3, bf16[32,2,32,2,256,1]{4,2,1,0,3,5:T(8,128)(2,1)S(1)} %select_bitcast_fusion), kind=kOutput, calls=%fused_computation.4 | convolution fusion | flops 1092616192 | bytes 23068680 | tf_op jit(solution)/shard_map/wcktp,ewcktq->tekpq/dot_general | solution.py:29
  189.3 21.2 %copy.26 = bf16[1,1,2,2,32,256,256]{6,5,4,3,2,1,0:T(8,128)(2,1)} copy(bf16[1,1,2,2,32,256,256]{5,6,3,4,2,1,0:T(8,128)(2,1)} %fusion.1) | data formatting | bytes 33554432 | tf_op jit(solution)/shard_map/reshape | solution.py:58
  (11 shorter events, 0.1 us)
Async XLA Ops:
  6.5 33.9 %copy-start = (s32[1,1,4,2]{2,3,1,0:T(2,128)S(1)}, s32[1,1,4,2]{2,3,1,0:T(2,128)}, u32[]{:S(2)}) copy-start(s32[1,1,4,2]{2,3,1,0:T(2,128)} %param.7) | copy-start | bytes 100
  6.5 32.5 %all-gather.4.cloned.1.call-start = ((), (), s32[]{:S(2)}) async-start(), calls=%async_computation | async-start | bytes 1572864 | tf_op jit(solution)/shard_map/all_gather | solution.py:42
  14.9 106.3 %all-gather.6.cloned.1.call-start = ((), (), s32[]{:S(2)}) async-start(), calls=%async_computation.1 | async-start | bytes 5242880 | tf_op jit(solution)/shard_map/all_gather | solution.py:44
  39.0 116.9 %all-gather.8.cloned.1.call-start = ((), (), s32[]{:S(2)}) async-start(), calls=%async_computation.2 | async-start | bytes 5242880 | tf_op jit(solution)/shard_map/all_gather | solution.py:43
  178.3 1.2 copy-start.2
  179.5 1.6 copy-start.3
  189.3 21.2 %copy-start.1 = (s32[1,1,4,2]{2,3,1,0:T(2,128)S(1)}, s32[1,1,4,2]{2,3,1,0:T(2,128)}, u32[]{:S(2)}) copy-start(s32[1,1,4,2]{2,3,1,0:T(2,128)} %param.7) | copy-start | bytes 100
Sparse Core Ops, SparseCore 0:
  15.0 23.9 all-gather.3
  40.6 80.5 all-gather.5
  122.7 33.1 all-gather.7
where the time goes:
time: 218 us; the launch traced here: 217 us
  waiting for transfers between devices  127 us (58%)
  local copies, waits for them, and re-layouts  55.6 us (26%)
  matrix products  14.3 us (7%)
  between operations  13.9 us (6%)
  other arithmetic  6.51 us (3%)
    all_gather x1, waiting for transfers between devices, body(): column_set = lax.all_gather(whitened, 'row', axis=2, tiled=True)  80.3 us
    all_gather x1, waiting for transfers between devices, body(): whitened = lax.all_gather(whitened, 'win', axis=0, tiled=True)  24.1 us
    all_gather x1, waiting for transfers between devices, body(): row_set = lax.all_gather(whitened, 'col', axis=2, tiled=True)  21.6 us
    reshape x1, local copies, waits for them, and re-layouts, body(): summed.astype(jnp.bfloat16)  21.2 us
    reshape x2, local copies, waits for them, and re-layouts, body(): column_set.reshape(window_rows, 2, kept_bins, lax.axis_size('row'), chan_...  13.2 us
    reshape x2, local copies, waits for them, and re-layouts, body(): row_set.reshape(window_rows, 2, kept_bins, lax.axis_size('col'), chan_block)  12.8 us
    dot_general x1, matrix products, cross_spectra(): jnp.einsum('wcktp,ewcktq->tekpq', first_block, stacked, preferred_element...  8.24 us
    dot_general x1, matrix products, body(): jnp.einsum('wcs,sk->wkc', records, phase_table, preferred_element_type=jn...  6.06 us
  transfers between devices with their start and end apart: 3, of which 3 were waited for; matrix products, arithmetic and copies ran while one was open for 6% of the time, Pallas kernels for 0%

commit v1 on v0

v1 whole, which is shorter than its diff:
```python
import functools
import math

import jax
import jax.numpy as jnp
from jax import lax
from jax.experimental import pallas as pl
from jax.experimental.pallas import tpu as pltpu
from jax.sharding import PartitionSpec as P

GROUP = 8
UP, DOWN, PARTNER, RIGHT, LEFT, SIBLING = range(6)


def dft_table(bin_index, length):
    sample_ids = jnp.arange(length, dtype=jnp.int32)
    phases = sample_ids[:, None] * bin_index[None, :] % length
    angles = 2.0 * math.pi / length * phases.astype(jnp.float32)
    window_taper = 0.5 - 0.5 * jnp.cos(2.0 * math.pi / length * sample_ids.astype(jnp.float32))
    cosine = window_taper[:, None] * jnp.cos(angles)
    sine = -window_taper[:, None] * jnp.sin(angles)
    table = jnp.stack([cosine, sine], axis=2).astype(jnp.bfloat16)
    return table.reshape(length, -1).T


def gather_kernel(rows, cols, groups, rec_hbm, basis_ref, sets, rec, spec, own,
                  rec_sem, local_sem, send_sem, recv_sem):
    w, r, q = lax.axis_index("win"), lax.axis_index("row"), lax.axis_index("col")
    chips = cols // 2
    x = q // 2
    other = 1 - w
    sib = q + 1 - 2 * (q % 2)
    mine, theirs = w * groups, other * groups
    device = {
        UP: (w, r + 1, q), DOWN: (w, r - 1, q), PARTNER: (other, r, q),
        RIGHT: (w, r, q + 2), LEFT: (w, r, q - 2), SIBLING: (w, r, sib),
    }
    exists = {
        UP: r < rows - 1, DOWN: r > 0, PARTNER: None,
        RIGHT: x < chips - 1, LEFT: x > 0, SIBLING: None,
    }

    def fetch(i):
        part = pl.ds(i * GROUP, GROUP)
        return pltpu.make_async_copy(rec_hbm.at[part], rec.at[part], rec_sem.at[i])

    for i in range(groups):
        fetch(i).start()

    def guarded(way, f):
        if exists[way] is None:
            f()
        else:
            pl.when(exists[way])(f)

    barrier = pltpu.get_barrier_semaphore()
    for way in range(6):
        guarded(way, lambda way=way: pl.semaphore_signal(
            barrier, inc=1, device_id=device[way], device_id_type=pl.DeviceIdType.MESH))
    ends = sum(exists[way].astype(jnp.int32) for way in (UP, DOWN, RIGHT, LEFT))
    pl.semaphore_wait(barrier, 2 + ends)

    def copy(way, src, slot, g):
        return pltpu.make_async_remote_copy(
            src_ref=src, dst_ref=sets.at[slot, g], send_sem=send_sem.at[way, slot, g],
            recv_sem=recv_sem.at[slot, g], device_id=device[way],
            device_id_type=pl.DeviceIdType.MESH)

    pending = []

    def send(way, src, slot, g, cond=None):
        def go():
            guarded(way, lambda: copy(way, src, slot, g).start())

        def done():
            guarded(way, lambda: copy(way, src, slot, g).wait_send())

        if cond is None:
            go()
        pending.append((cond, done))
        return go

    def arrived(slot, g):
        copy(PARTNER, sets.at[slot, g], slot, g).wait_recv()

    keeps = []
    for i in range(groups):
        fetch(i).wait()

        def one_window(v, _, i=i):
            s = lax.dot_general(basis_ref[...], rec[i * GROUP + v], (((1,), (1,)), ((), ())),
                                preferred_element_type=jnp.float32)
            scale = 1.0 / jnp.sqrt(jnp.mean(s * s, axis=0, keepdims=True) + 1e-06)
            s = s * scale
            for lane in range(spec.shape[0]):
                spec[lane, pl.ds(v, s.shape[0], stride=GROUP), :] = s[:, lane * 128:(lane + 1) * 128]
            return 0

        lax.fori_loop(0, GROUP, one_window, 0)
        for lane in range(spec.shape[0]):
            own[i, :, :, lane * 128:(lane + 1) * 128] = spec[lane].astype(jnp.bfloat16).reshape(
                own.shape[1], own.shape[2], 128)
        for way in (PARTNER, UP, DOWN):
            send(way, own.at[i], r, mine + i)
        for way in (RIGHT, LEFT, SIBLING):
            send(way, own.at[i], rows + q, mine + i)
        keep = pltpu.make_async_copy(own.at[i], sets.at[r, mine + i], local_sem.at[i])
        keep.start()
        keeps.append(keep)

    def relay(cond, slot, g, ways):
        goes = [send(way, sets.at[slot, g], slot, g, cond) for way in ways]

        def go():
            arrived(slot, g)
            for f in goes:
                f()

        pl.when(cond)(go)

    def along_x(g):
        for d in range(1, chips):
            relay(x - d >= 0, rows + q - 2 * d, g, (RIGHT, SIBLING))
            relay(x + d < chips, rows + q + 2 * d, g, (LEFT, SIBLING))

    for h in range(1, rows):
        for i in range(groups):
            if h == 1:
                arrived(r, theirs + i)
                for way in (RIGHT, LEFT, SIBLING):
                    send(way, sets.at[r, theirs + i], rows + q, theirs + i)
            relay(r - h >= 0, r - h, mine + i, (UP, PARTNER))
            relay(r + h < rows, r + h, mine + i, (DOWN, PARTNER))
        if h == 1:
            for i in range(groups):
                along_x(mine + i)
    for i in range(groups):
        along_x(theirs + i)

    for h in range(1, rows):
        for i in range(groups):
            pl.when(r - h >= 0)(lambda h=h, i=i: arrived(r - h, theirs + i))
            pl.when(r + h < rows)(lambda h=h, i=i: arrived(r + h, theirs + i))
    for c in range(chips):
        for g in range(2 * groups):
            arrived(rows + 2 * c + 1 - q % 2, g)
    for keep in keeps:
        keep.wait()
    for cond, done in pending:
        if cond is None:
            done()
        else:
            pl.when(cond)(done)


def gather(records, table, rows, cols):
    windows, channels, length = records.shape
    groups = windows // GROUP
    entries = table.shape[0]
    bins = entries // 2
    slots = rows + cols
    return pl.pallas_call(
        functools.partial(gather_kernel, rows, cols, groups),
        out_shape=jax.ShapeDtypeStruct(
            (slots, 2 * groups, bins, 2 * GROUP, channels), jnp.bfloat16),
        in_specs=[pl.BlockSpec(memory_space=pl.ANY), pl.BlockSpec(memory_space=pltpu.VMEM)],
        out_specs=pl.BlockSpec(memory_space=pl.ANY),
        scratch_shapes=[
            pltpu.VMEM(records.shape, jnp.bfloat16),
            pltpu.VMEM((channels // 128, entries * GROUP, 128), jnp.float32),
            pltpu.VMEM((groups, bins, 2 * GROUP, channels), jnp.bfloat16),
            pltpu.SemaphoreType.DMA((groups,)),
            pltpu.SemaphoreType.DMA((groups,)),
            pltpu.SemaphoreType.DMA((6, slots, 2 * groups)),
            pltpu.SemaphoreType.DMA((slots, 2 * groups)),
        ],
        compiler_params=pltpu.CompilerParams(
            collective_id=0, has_side_effects=True, vmem_limit_bytes=40 * 2**20),
        cost_estimate=pl.CostEstimate(
            flops=2 * windows * channels * length * entries,
            bytes_accessed=windows * channels * length * 2, transcendentals=0),
    )(records, table)


def cross_kernel(picks, first, second, out):
    slot = pl.program_id(0)
    live = picks[slot, 2] != 0

    @pl.when(live)
    def _():
        for k in range(first.shape[2]):
            a = first[0, :, k].reshape(-1, first.shape[4])
            b = second[0, :, k].reshape(a.shape)
            parts = b.astype(jnp.float32).reshape(first.shape[1], 2, GROUP, a.shape[1])
            turned = jnp.concatenate([-parts[:, 1:], parts[:, :1]], axis=1)
            turned = turned.reshape(a.shape).astype(jnp.bfloat16)
            for e, m in enumerate((b, turned)):
                out[0, 0, 0, e, k] = lax.dot_general(
                    a, m, (((0,), (0,)), ((), ())), preferred_element_type=jnp.float32
                ).astype(jnp.bfloat16)

    @pl.when(jnp.logical_not(live))
    def _():
        out[...] = jnp.zeros_like(out)


def cross(sets, picks):
    _, groups, bins, pairs, channels = sets.shape
    owned = picks.shape[0]
    step = math.gcd(bins, 4)
    block = (1, groups, step, pairs, channels)
    return pl.pallas_call(
        cross_kernel,
        out_shape=jax.ShapeDtypeStruct(
            (1, 1, owned, 2, bins, channels, channels), jnp.bfloat16),
        grid_spec=pltpu.PrefetchScalarGridSpec(
            num_scalar_prefetch=1,
            grid=(owned, bins // step),
            in_specs=[
                pl.BlockSpec(block, lambda s, k, p: (p[s, 0], 0, k, 0, 0)),
                pl.BlockSpec(block, lambda s, k, p: (p[s, 1], 0, k, 0, 0)),
            ],
            out_specs=pl.BlockSpec(
                (1, 1, 1, 2, step, channels, channels), lambda s, k, p: (0, 0, s, 0, k, 0, 0)),
        ),
        compiler_params=pltpu.CompilerParams(vmem_limit_bytes=40 * 2**20),
        cost_estimate=pl.CostEstimate(
            flops=4 * owned * bins * channels * channels * groups * pairs,
            bytes_accessed=4 * owned * bins * channels * channels, transcendentals=0),
    )(picks, sets, sets)


def body(records, tile_pairs, tile_count, bin_index):
    rows, cols = lax.axis_size("row"), lax.axis_size("col")
    r, q = lax.axis_index("row"), lax.axis_index("col")
    table = dft_table(bin_index, records.shape[2])
    sets = gather(records, table, rows, cols)
    owned = tile_pairs.shape[2] // lax.axis_size("win")
    begin = lax.axis_index("win") * owned
    chosen = lax.dynamic_slice_in_dim(tile_pairs[0, 0], begin, owned, 0)
    live = (begin + jnp.arange(owned, dtype=jnp.int32) < tile_count[0, 0]).astype(jnp.int32)
    first = jnp.where(chosen[:, 0] == q, r, rows + chosen[:, 0])
    picks = jnp.stack([first, chosen[:, 1], live], axis=1).astype(jnp.int32)
    return cross(sets, picks)


def solution(mesh):
    return jax.shard_map(
        body,
        mesh=mesh,
        in_specs=(
            P("win", ("row", "col"), None),
            P("row", "col", None, None),
            P("row", "col"),
            P(),
        ),
        out_specs=P("row", "col", "win", None, None, None, None),
        check_vma=False,
    )
```

time: 218 us -> 71 us (0.33)
  waiting for transfers between devices: 127 us -> 0 us
  Pallas kernels: 0 us -> 68.3 us
  local copies, waits for them, and re-layouts: 55.6 us -> 0.37 us
  matrix products: 14.3 us -> 0 us
  between operations: 13.9 us -> 0.72 us
  other arithmetic: 6.51 us -> 1.48 us
    all_gather x3 -> x0, waiting for transfers between devices: 126 us -> none  [the longest x1 80.3 us: body(): column_set = lax.all_gather(whitened, 'row', axis=2, tiled=True)]
    pallas_call x0 -> x2, Pallas kernels: none -> 68.3 us  [the longest x1 55.5 us: gather(): pl.pallas_call(functools.partial(gather_kernel, rows, cols, groups), out_...]
    reshape x5 -> x0, local copies, waits for them, and re-layouts: 47.2 us -> none  [the longest x1 21.2 us: body(): summed.astype(jnp.bfloat16)]
    dot_general x2 -> x0, matrix products: 14.3 us -> none  [the longest x1 8.24 us: cross_spectra(): jnp.einsum('wcktp,ewcktq->tekpq', first_block, stacked, preferred_element...]
    gather x2 -> x0, local copies, waits for them, and re-layouts: 5.73 us -> none  [the longest x1 2.87 us: body(): second_chosen = jnp.take(column_blocks, chosen[:, 1], axis=3)]
    another operation x3, other arithmetic: 4.15 us -> 1.35 us  [the longest x2 2.89 us: cross_spectra(): jnp.stack([jnp.stack([second_real, second_imag], axis=1), jnp.stack([-sec...]
    unnamed x8 -> x2, local copies, waits for them, and re-layouts: 2.31 us -> 0.01 us
  transfers between devices with their start and end apart: 3 -> 0, of which waited for: 3 -> 0; matrix products, arithmetic and copies ran while one was open for 6% -> 0% of each run, Pallas kernels for 0% -> 0%
where the time goes in v1:
time: 71 us; the launch traced here: 70.8 us
  Pallas kernels  68.3 us (96%)
  other arithmetic  1.48 us (2%)
  between operations  0.72 us (1%)
    pallas_call x1, Pallas kernels, gather(): pl.pallas_call(functools.partial(gather_kernel, rows, cols, groups), out_...  55.5 us
    pallas_call x1, Pallas kernels, cross(): pl.pallas_call(cross_kernel, out_shape=jax.ShapeDtypeStruct((1, 1, owned,...  12.7 us

profile of v1, /device:TPU:0, one launch (start us, length us, event | category | flops | bytes accessed | tf_op | source)
XLA Modules:
  0.0 70.8 jit_solution(7278053097583622900)
XLA Ops:
  0.0 0.0 copy-start
  0.7 0.0 copy-done
  0.7 0.1 constant_dynamic-slice_fusion
  0.8 0.1 copy.6
  0.9 0.1 compare_select_fusion
  0.9 0.1 pad_add_fusion.picks
  1.1 1.3 %multiply_convert_fusion.1 = (bf16[1024,32,1]{0,1,2:T(8,128)(2,1)S(1)}, bf16[1024,32,1]{0,1,2:T(8,128)(2,1)S(1)}) fusion(s32[32]{0:T(128)} %param.7, f32[1024]{0:T(1024)S(1)} %get-tuple-element.9, f32[1024]{0:T(1024)S(1)} %get-tuple-element.10), kind=kLoop, calls=%fused_computation.8 | loop fusion | flops 589824 | bytes 139392 | tf_op jit(solution)/shard_map/convert
  2.3 0.1 copy.7
  2.5 0.1 convert_element_type.44
  2.6 55.5 %shard_map.46.first.second = bf16[8,4,32,16,256]{4,3,2,1,0:T(8,128)(2,1)S(1)} custom-call(bf16[16,256,1024]{2,1,0:T(8,128)(2,1)} %rec_hbm.1, bf16[64,1024]{1,0:T(8,128)(2,1)S(1)} %bitcast.6), custom_call_target="tpu_custom_call" | custom-call | flops 536870912 | bytes 8388608 | tf_op jit(solution)/shard_map/pallas_call | solution.py:162
  58.1 12.7 %shard_map.47 = bf16[1,1,2,2,32,256,256]{6,5,4,3,2,1,0:T(8,128)(2,1)} custom-call(s32[2,3]{1,0:T(2,128)S(1)} %pad_add_fusion.picks, bf16[8,4,32,16,256]{4,3,2,1,0:T(8,128)(2,1)S(1)} %shard_map.46.first.second, bf16[8,4,32,16,256]{4,3,2,1,0:T(8,128)(2,1)S(1)} %shard_map.46.first.second), custom_call_target="tpu_custom_call" | custom-call | flops 1073741824 | bytes 16777216 | tf_op jit(solution)/shard_map/pallas_call | solution.py:212
  (3 shorter events, 0.1 us)
Async XLA Ops:
  0.0 0.7 copy-start

commit v2 on v1

--- a/solution.py
+++ b/solution.py
@@ -12,18 +12,17 @@
 UP, DOWN, PARTNER, RIGHT, LEFT, SIBLING = range(6)
 
 
-def dft_table(bin_index, length):
+def dft_tables(bin_index, length):
     sample_ids = jnp.arange(length, dtype=jnp.int32)
-    phases = sample_ids[:, None] * bin_index[None, :] % length
+    phases = bin_index[:, None] * sample_ids[None, :] % length
     angles = 2.0 * math.pi / length * phases.astype(jnp.float32)
     window_taper = 0.5 - 0.5 * jnp.cos(2.0 * math.pi / length * sample_ids.astype(jnp.float32))
-    cosine = window_taper[:, None] * jnp.cos(angles)
-    sine = -window_taper[:, None] * jnp.sin(angles)
-    table = jnp.stack([cosine, sine], axis=2).astype(jnp.bfloat16)
-    return table.reshape(length, -1).T
-
-
-def gather_kernel(rows, cols, groups, rec_hbm, basis_ref, sets, rec, spec, own,
+    cosine = window_taper[None, :] * jnp.cos(angles)
+    sine = -window_taper[None, :] * jnp.sin(angles)
+    return cosine.astype(jnp.bfloat16), sine.astype(jnp.bfloat16)
+
+
+def gather_kernel(rows, cols, groups, rec_hbm, cos_ref, sin_ref, sets, rec, spec, own,
                   rec_sem, local_sem, send_sem, recv_sem):
     w, r, q = lax.axis_index("win"), lax.axis_index("row"), lax.axis_index("col")
     chips = cols // 2
@@ -83,17 +82,21 @@
     def arrived(slot, g):
         copy(PARTNER, sets.at[slot, g], slot, g).wait_recv()
 
+    bins = cos_ref.shape[0]
     keeps = []
     for i in range(groups):
         fetch(i).wait()
 
         def one_window(v, _, i=i):
-            s = lax.dot_general(basis_ref[...], rec[i * GROUP + v], (((1,), (1,)), ((), ())),
+            table = jnp.concatenate([cos_ref[...], sin_ref[...]], axis=0)
+            s = lax.dot_general(table, rec[i * GROUP + v], (((1,), (1,)), ((), ())),
                                 preferred_element_type=jnp.float32)
             scale = 1.0 / jnp.sqrt(jnp.mean(s * s, axis=0, keepdims=True) + 1e-06)
             s = s * scale
             for lane in range(spec.shape[0]):
-                spec[lane, pl.ds(v, s.shape[0], stride=GROUP), :] = s[:, lane * 128:(lane + 1) * 128]
+                part = s[:, lane * 128:(lane + 1) * 128]
+                spec[lane, pl.ds(v, bins, stride=2 * GROUP), :] = part[:bins]
+                spec[lane, pl.ds(v + GROUP, bins, stride=2 * GROUP), :] = part[bins:]
             return 0
 
         lax.fori_loop(0, GROUP, one_window, 0)
@@ -129,8 +132,12 @@
                 arrived(r, theirs + i)
                 for way in (RIGHT, LEFT, SIBLING):
                     send(way, sets.at[r, theirs + i], rows + q, theirs + i)
-            relay(r - h >= 0, r - h, mine + i, (UP, PARTNER))
-            relay(r + h < rows, r + h, mine + i, (DOWN, PARTNER))
+                if i == groups - 1:
+                    for way in (UP, DOWN):
+                        send(way, sets.at[r, theirs + i], r, theirs + i)
+            shared = () if h == 1 and i == groups - 1 else (PARTNER,)
+            relay(r - h >= 0, r - h, mine + i, (UP,) + shared)
+            relay(r + h < rows, r + h, mine + i, (DOWN,) + shared)
         if h == 1:
             for i in range(groups):
                 along_x(mine + i)
@@ -153,17 +160,17 @@
             pl.when(cond)(done)
 
 
-def gather(records, table, rows, cols):
+def gather(records, tables, rows, cols):
     windows, channels, length = records.shape
     groups = windows // GROUP
-    entries = table.shape[0]
+    entries = 2 * tables[0].shape[0]
     bins = entries // 2
     slots = rows + cols
     return pl.pallas_call(
         functools.partial(gather_kernel, rows, cols, groups),
         out_shape=jax.ShapeDtypeStruct(
             (slots, 2 * groups, bins, 2 * GROUP, channels), jnp.bfloat16),
-        in_specs=[pl.BlockSpec(memory_space=pl.ANY), pl.BlockSpec(memory_space=pltpu.VMEM)],
+        in_specs=[pl.BlockSpec(memory_space=pl.ANY)] + [pl.BlockSpec(memory_space=pltpu.VMEM)] * 2,
         out_specs=pl.BlockSpec(memory_space=pl.ANY),
         scratch_shapes=[
             pltpu.VMEM(records.shape, jnp.bfloat16),
@@ -179,12 +186,11 @@
         cost_estimate=pl.CostEstimate(
             flops=2 * windows * channels * length * entries,
             bytes_accessed=windows * channels * length * 2, transcendentals=0),
-    )(records, table)
-
-
-def cross_kernel(picks, first, second, out):
-    slot = pl.program_id(0)
-    live = picks[slot, 2] != 0
+    )(records, *tables)
+
+
+def cross_kernel(pairs, count, place, first, second, out):
+    live = place[0] + pl.program_id(0) < count[0]
 
     @pl.when(live)
     def _():
@@ -204,44 +210,46 @@
         out[...] = jnp.zeros_like(out)
 
 
-def cross(sets, picks):
-    _, groups, bins, pairs, channels = sets.shape
-    owned = picks.shape[0]
+def cross(sets, pairs, count, place, rows, owned):
+    _, groups, bins, entries, channels = sets.shape
     step = math.gcd(bins, 4)
-    block = (1, groups, step, pairs, channels)
+    block = (1, groups, step, entries, channels)
+
+    def first_map(s, k, pairs, count, place):
+        i = pairs[2 * (place[0] + s)]
+        return jnp.where(i == place[2], place[1], rows + i), 0, k, 0, 0
+
+    def second_map(s, k, pairs, count, place):
+        return pairs[2 * (place[0] + s) + 1], 0, k, 0, 0
+
     return pl.pallas_call(
         cross_kernel,
         out_shape=jax.ShapeDtypeStruct(
             (1, 1, owned, 2, bins, channels, channels), jnp.bfloat16),
         grid_spec=pltpu.PrefetchScalarGridSpec(
-            num_scalar_prefetch=1,
+            num_scalar_prefetch=3,
             grid=(owned, bins // step),
             in_specs=[
-                pl.BlockSpec(block, lambda s, k, p: (p[s, 0], 0, k, 0, 0)),
-                pl.BlockSpec(block, lambda s, k, p: (p[s, 1], 0, k, 0, 0)),
+                pl.BlockSpec(block, first_map),
+                pl.BlockSpec(block, second_map),
             ],
             out_specs=pl.BlockSpec(
-                (1, 1, 1, 2, step, channels, channels), lambda s, k, p: (0, 0, s, 0, k, 0, 0)),
+                (1, 1, 1, 2, step, channels, channels), lambda s, k, *_: (0, 0, s, 0, k, 0, 0)),
         ),
         compiler_params=pltpu.CompilerParams(vmem_limit_bytes=40 * 2**20),
         cost_estimate=pl.CostEstimate(
-            flops=4 * owned * bins * channels * channels * groups * pairs,
+            flops=4 * owned * bins * channels * channels * groups * entries,
             bytes_accessed=4 * owned * bins * channels * channels, transcendentals=0),
-    )(picks, sets, sets)
+    )(pairs, count, place, sets, sets)
 
 
 def body(records, tile_pairs, tile_count, bin_index):
     rows, cols = lax.axis_size("row"), lax.axis_size("col")
     r, q = lax.axis_index("row"), lax.axis_index("col")
-    table = dft_table(bin_index, records.shape[2])
-    sets = gather(records, table, rows, cols)
+    sets = gather(records, dft_tables(bin_index, records.shape[2]), rows, cols)
     owned = tile_pairs.shape[2] // lax.axis_size("win")
-    begin = lax.axis_index("win") * owned
-    chosen = lax.dynamic_slice_in_dim(tile_pairs[0, 0], begin, owned, 0)
-    live = (begin + jnp.arange(owned, dtype=jnp.int32) < tile_count[0, 0]).astype(jnp.int32)
-    first = jnp.where(chosen[:, 0] == q, r, rows + chosen[:, 0])
-    picks = jnp.stack([first, chosen[:, 1], live], axis=1).astype(jnp.int32)
-    return cross(sets, picks)
+    place = jnp.stack([lax.axis_index("win") * owned, r, q]).astype(jnp.int32)
+    return cross(sets, tile_pairs.reshape(-1), tile_count.reshape(-1), place, rows, owned)
 
 
 def solution(mesh):

time: 71 us -> 72.4 us (1.020); the launches traced: 70.8 us -> 73 us
  Pallas kernels: 68.3 us -> 70.1 us
    pallas_call x1, Pallas kernels: 55.5 us -> 57.3 us  [gather(): pl.pallas_call(functools.partial(gather_kernel, rows, cols, groups), out_...]
    another operation x3 -> x1, other arithmetic: 1.35 us -> 0.08 us  [body(): place = jnp.stack([lax.axis_index('win') * owned, r, q]).astype(jnp.int32)]
    convert_element_type x1, other arithmetic: 0.01 us -> 1.26 us  [dft_tables(): return (cosine.astype(jnp.bfloat16), sine.astype(jnp.bfloat16))]
    unnamed x2 -> x1, local copies, waits for them, and re-layouts: 0.01 us -> 0.77 us
where the time goes in v2:
time: 72.4 us; the launch traced here: 73 us
  Pallas kernels  70.1 us (97%)
  other arithmetic  1.38 us (2%)
  local copies, waits for them, and re-layouts  0.85 us (1%)
    pallas_call x1, Pallas kernels, gather(): pl.pallas_call(functools.partial(gather_kernel, rows, cols, groups), out_...  57.3 us
    pallas_call x1, Pallas kernels, cross(): pl.pallas_call(cross_kernel, out_shape=jax.ShapeDtypeStruct((1, 1, owned,...  12.8 us

profile of v2, /device:TPU:0, one launch (start us, length us, event | category | flops | bytes accessed | tf_op | source)
XLA Modules:
  0.0 73.0 jit_solution(2936532345289048334)
XLA Ops:
  0.7 0.1 pad_add_fusion.place
  0.7 0.8 %copy.6 = s32[1,1,4,2]{3,2,1,0:T(4,128)S(1)} copy(s32[1,1,4,2]{2,3,1,0:T(2,128)} %param.5) | data formatting | bytes 64 | tf_op args[1]
  1.5 0.1 reshape.19.pairs
  1.6 1.3 %multiply_convert_fusion = (bf16[32,1024]{1,0:T(8,128)(2,1)S(1)}, bf16[32,1024]{1,0:T(8,128)(2,1)S(1)}) fusion(f32[1024]{0:T(1024)S(1)} %get-tuple-element.8, s32[32]{0:T(128)} %param.7, f32[1024]{0:T(1024)S(1)} %get-tuple-element.7), kind=kLoop, calls=%fused_computation.6 | loop fusion | flops 589824 | bytes 139392 | tf_op jit(solution)/shard_map/convert_element_type | solution.py:22
  2.9 57.3 %shard_map.46.first.second = bf16[8,4,32,16,256]{4,3,2,1,0:T(8,128)(2,1)S(1)} custom-call(bf16[16,256,1024]{2,1,0:T(8,128)(2,1)} %rec_hbm.1, bf16[32,1024]{1,0:T(8,128)(2,1)S(1)} %get-tuple-element.6.cos_ref, bf16[32,1024]{1,0:T(8,128)(2,1)S(1)} %get-tuple-element.5.sin_ref), custom_call_target="tpu_custom_call" | custom-call | flops 536870912 | bytes 8388608 | tf_op jit(solution)/shard_map/pallas_call | solution.py:169
  60.2 12.8 %shard_map.47 = bf16[1,1,2,2,32,256,256]{6,5,4,3,2,1,0:T(8,128)(2,1)} custom-call(s32[8]{0:T(128)S(1)} %reshape.19.pairs, s32[1]{0:T(128)} %bitcast.4.count, s32[3]{0:T(128)S(1)} %pad_add_fusion.place, bf16[8,4,32,16,256]{4,3,2,1,0:T(8,128)(2,1)S(1)} %shard_map.46.first.second, bf16[8,4,32,16,256]{4,3,2,1,0:T(8,128)(2,1)S(1)} %shard_map.46.first.second), custom_call_target="tpu_custom_call" | custom-call | flops 1073741824 | bytes 16777216 | tf_op jit(solution)/shard_map/pallas_call | solution.py:225
  (1 shorter events, 0.0 us)

commit v3 on v2

--- a/solution.py
+++ b/solution.py
@@ -132,15 +132,14 @@
                 arrived(r, theirs + i)
                 for way in (RIGHT, LEFT, SIBLING):
                     send(way, sets.at[r, theirs + i], rows + q, theirs + i)
-                if i == groups - 1:
-                    for way in (UP, DOWN):
-                        send(way, sets.at[r, theirs + i], r, theirs + i)
             shared = () if h == 1 and i == groups - 1 else (PARTNER,)
             relay(r - h >= 0, r - h, mine + i, (UP,) + shared)
             relay(r + h < rows, r + h, mine + i, (DOWN,) + shared)
         if h == 1:
             for i in range(groups):
                 along_x(mine + i)
+    for way in (UP, DOWN):
+        send(way, sets.at[r, theirs + groups - 1], r, theirs + groups - 1)
     for i in range(groups):
         along_x(theirs + i)
 
@@ -189,58 +188,74 @@
     )(records, *tables)
 
 
-def cross_kernel(pairs, count, place, first, second, out):
-    live = place[0] + pl.program_id(0) < count[0]
-
-    @pl.when(live)
-    def _():
-        for k in range(first.shape[2]):
-            a = first[0, :, k].reshape(-1, first.shape[4])
-            b = second[0, :, k].reshape(a.shape)
-            parts = b.astype(jnp.float32).reshape(first.shape[1], 2, GROUP, a.shape[1])
-            turned = jnp.concatenate([-parts[:, 1:], parts[:, :1]], axis=1)
-            turned = turned.reshape(a.shape).astype(jnp.bfloat16)
-            for e, m in enumerate((b, turned)):
-                out[0, 0, 0, e, k] = lax.dot_general(
-                    a, m, (((0,), (0,)), ((), ())), preferred_element_type=jnp.float32
-                ).astype(jnp.bfloat16)
-
-    @pl.when(jnp.logical_not(live))
-    def _():
-        out[...] = jnp.zeros_like(out)
+def cross_kernel(rows, owned, pairs, count, place, sets, out, ring, sem):
+    depth, _, step, channels, _ = ring.shape
+    groups = sets.shape[1]
+    chunks = out.shape[4] // step
+
+    def copy(n):
+        part = pl.ds((n % chunks) * step, step)
+        return pltpu.make_async_copy(
+            ring.at[n % depth], out.at[0, 0, n // chunks, :, part], sem.at[n % depth])
+
+    def one(n, _):
+        slot = n % depth
+        position = place[0] + n // chunks
+        i, j = pairs[2 * position], pairs[2 * position + 1]
+        first = jnp.where(i == place[2], place[1], rows + i)
+        live = position < count[0]
+
+        @pl.when(n >= depth)
+        def _():
+            copy(n - depth).wait()
+
+        @pl.when(live)
+        def _():
+            for t in range(step):
+                k = (n % chunks) * step + t
+                a = sets[first, :, k].reshape(-1, channels)
+                b = sets[j, :, k].reshape(a.shape)
+                parts = b.astype(jnp.float32).reshape(groups, 2, GROUP, channels)
+                turned = jnp.concatenate([-parts[:, 1:], parts[:, :1]], axis=1)
+                turned = turned.reshape(a.shape).astype(jnp.bfloat16)
+                both = lax.dot_general(
+                    a, jnp.concatenate([b, turned], axis=1), (((0,), (0,)), ((), ())),
+                    preferred_element_type=jnp.float32)
+                ring[slot, 0, t] = both[:, :channels].astype(jnp.bfloat16)
+                ring[slot, 1, t] = both[:, channels:].astype(jnp.bfloat16)
+
+        @pl.when(jnp.logical_not(live))
+        def _():
+            ring[slot] = jnp.zeros(ring.shape[1:], jnp.bfloat16)
+
+        copy(n).start()
+        return 0
+
+    total = owned * chunks
+    lax.fori_loop(0, total, one, 0)
+    for n in range(max(total - depth, 0), total):
+        copy(n).wait()
 
 
 def cross(sets, pairs, count, place, rows, owned):
     _, groups, bins, entries, channels = sets.shape
     step = math.gcd(bins, 4)
-    block = (1, groups, step, entries, channels)
-
-    def first_map(s, k, pairs, count, place):
-        i = pairs[2 * (place[0] + s)]
-        return jnp.where(i == place[2], place[1], rows + i), 0, k, 0, 0
-
-    def second_map(s, k, pairs, count, place):
-        return pairs[2 * (place[0] + s) + 1], 0, k, 0, 0
-
+    smem = pl.BlockSpec(memory_space=pltpu.SMEM)
     return pl.pallas_call(
-        cross_kernel,
+        functools.partial(cross_kernel, rows, owned),
         out_shape=jax.ShapeDtypeStruct(
             (1, 1, owned, 2, bins, channels, channels), jnp.bfloat16),
-        grid_spec=pltpu.PrefetchScalarGridSpec(
-            num_scalar_prefetch=3,
-            grid=(owned, bins // step),
-            in_specs=[
-                pl.BlockSpec(block, first_map),
-                pl.BlockSpec(block, second_map),
-            ],
-            out_specs=pl.BlockSpec(
-                (1, 1, 1, 2, step, channels, channels), lambda s, k, *_: (0, 0, s, 0, k, 0, 0)),
-        ),
+        in_specs=[smem, smem, smem, pl.BlockSpec(memory_space=pltpu.VMEM)],
+        out_specs=pl.BlockSpec(memory_space=pl.ANY),
+        scratch_shapes=[
+            pltpu.VMEM((4, 2, step, channels, channels), jnp.bfloat16),
+            pltpu.SemaphoreType.DMA((4,)),
+        ],
         compiler_params=pltpu.CompilerParams(vmem_limit_bytes=40 * 2**20),
         cost_estimate=pl.CostEstimate(
             flops=4 * owned * bins * channels * channels * groups * entries,
             bytes_accessed=4 * owned * bins * channels * channels, transcendentals=0),
-    )(pairs, count, place, sets, sets)
+    )(pairs, count, place, sets)
 
 
 def body(records, tile_pairs, tile_count, bin_index):

time: 72.4 us -> 62.7 us (0.87); the launches traced: 73 us -> 62.5 us
  Pallas kernels: 70.1 us -> 59.6 us
    pallas_call x1, Pallas kernels: 57.3 us -> 51.7 us  [gather(): pl.pallas_call(functools.partial(gather_kernel, rows, cols, groups), out_...]
    pallas_call x1, Pallas kernels: 12.8 us -> 7.91 us  [cross(): pl.pallas_call(functools.partial(cross_kernel, rows, owned), out_shape=ja...]
where the time goes in v3:
time: 62.7 us; the launch traced here: 62.5 us
  Pallas kernels  59.6 us (95%)
  other arithmetic  1.38 us (2%)
  local copies, waits for them, and re-layouts  0.85 us (1%)
  between operations  0.66 us (1%)
    pallas_call x1, Pallas kernels, gather(): pl.pallas_call(functools.partial(gather_kernel, rows, cols, groups), out_...  51.7 us
    pallas_call x1, Pallas kernels, cross(): pl.pallas_call(functools.partial(cross_kernel, rows, owned), out_shape=ja...  7.91 us
    convert_element_type x1, other arithmetic, dft_tables(): return (cosine.astype(jnp.bfloat16), sine.astype(jnp.bfloat16))  1.26 us

profile of v3, /device:TPU:0, one launch (start us, length us, event | category | flops | bytes accessed | tf_op | source)
XLA Modules:
  0.0 62.5 jit_solution(10947429822347624029)
XLA Ops:
  0.7 0.1 pad_add_fusion.place
  0.7 0.8 %copy.6 = s32[1,1,4,2]{3,2,1,0:T(4,128)S(1)} copy(s32[1,1,4,2]{2,3,1,0:T(2,128)} %param.5) | data formatting | bytes 64 | tf_op args[1]
  1.5 0.1 reshape.19.pairs
  1.6 1.3 %multiply_convert_fusion = (bf16[32,1024]{1,0:T(8,128)(2,1)S(1)}, bf16[32,1024]{1,0:T(8,128)(2,1)S(1)}) fusion(f32[1024]{0:T(1024)S(1)} %get-tuple-element.8, s32[32]{0:T(128)} %param.7, f32[1024]{0:T(1024)S(1)} %get-tuple-element.7), kind=kLoop, calls=%fused_computation.6 | loop fusion | flops 589824 | bytes 139392 | tf_op jit(solution)/shard_map/convert_element_type | solution.py:22
  2.9 51.7 %shard_map.46.sets = bf16[8,4,32,16,256]{4,3,2,1,0:T(8,128)(2,1)S(1)} custom-call(bf16[16,256,1024]{2,1,0:T(8,128)(2,1)} %rec_hbm.1, bf16[32,1024]{1,0:T(8,128)(2,1)S(1)} %get-tuple-element.6.cos_ref, bf16[32,1024]{1,0:T(8,128)(2,1)S(1)} %get-tuple-element.5.sin_ref), custom_call_target="tpu_custom_call" | custom-call | flops 536870912 | bytes 8388608 | tf_op jit(solution)/shard_map/pallas_call | solution.py:168
  54.6 7.9 %shard_map.47 = bf16[1,1,2,2,32,256,256]{6,5,4,3,2,1,0:T(8,128)(2,1)} custom-call(s32[8]{0:T(128)S(1)} %reshape.19.pairs, s32[1]{0:T(128)} %bitcast.4.count, s32[3]{0:T(128)S(1)} %pad_add_fusion.place, bf16[8,4,32,16,256]{4,3,2,1,0:T(8,128)(2,1)S(1)} %shard_map.46.sets), custom_call_target="tpu_custom_call" | custom-call | flops 1073741824 | bytes 16777216 | tf_op jit(solution)/shard_map/pallas_call | solution.py:244
  (1 shorter events, 0.0 us)

commit v4 on v3

--- a/solution.py
+++ b/solution.py
@@ -99,7 +99,7 @@
                 spec[lane, pl.ds(v + GROUP, bins, stride=2 * GROUP), :] = part[bins:]
             return 0
 
-        lax.fori_loop(0, GROUP, one_window, 0)
+        lax.fori_loop(0, GROUP, one_window, 0, unroll=4)
         for lane in range(spec.shape[0]):
             own[i, :, :, lane * 128:(lane + 1) * 128] = spec[lane].astype(jnp.bfloat16).reshape(
                 own.shape[1], own.shape[2], 128)
@@ -126,22 +126,29 @@
             relay(x - d >= 0, rows + q - 2 * d, g, (RIGHT, SIBLING))
             relay(x + d < chips, rows + q + 2 * d, g, (LEFT, SIBLING))
 
+    def extra(up, down):
+        g = theirs + groups - 1
+        for way, cond in ((UP, up), (DOWN, down)):
+            pl.when(cond)(send(way, sets.at[r, g], r, g, cond))
+
     for h in range(1, rows):
         for i in range(groups):
             if h == 1:
                 arrived(r, theirs + i)
                 for way in (RIGHT, LEFT, SIBLING):
                     send(way, sets.at[r, theirs + i], rows + q, theirs + i)
+            if h == 1 and i == groups - 1:
+                extra(r < rows - 2, r > 1)
             shared = () if h == 1 and i == groups - 1 else (PARTNER,)
             relay(r - h >= 0, r - h, mine + i, (UP,) + shared)
             relay(r + h < rows, r + h, mine + i, (DOWN,) + shared)
         if h == 1:
             for i in range(groups):
                 along_x(mine + i)
-    for way in (UP, DOWN):
-        send(way, sets.at[r, theirs + groups - 1], r, theirs + groups - 1)
-    for i in range(groups):
-        along_x(theirs + i)
+        if h == max(1, rows - 2):
+            for i in range(groups):
+                along_x(theirs + i)
+    extra(r == rows - 2, r == 1)
 
     for h in range(1, rows):
         for i in range(groups):
@@ -201,7 +208,7 @@
     def one(n, _):
         slot = n % depth
         position = place[0] + n // chunks
-        i, j = pairs[2 * position], pairs[2 * position + 1]
+        i, j = pairs[0, 0, 0, position], pairs[0, 0, 1, position]
         first = jnp.where(i == place[2], place[1], rows + i)
         live = position < count[0]
 
@@ -264,7 +271,7 @@
     sets = gather(records, dft_tables(bin_index, records.shape[2]), rows, cols)
     owned = tile_pairs.shape[2] // lax.axis_size("win")
     place = jnp.stack([lax.axis_index("win") * owned, r, q]).astype(jnp.int32)
-    return cross(sets, tile_pairs.reshape(-1), tile_count.reshape(-1), place, rows, owned)
+    return cross(sets, jnp.swapaxes(tile_pairs, 2, 3), tile_count.reshape(-1), place, rows, owned)
 
 
 def solution(mesh):

time: 62.7 us -> 64 us (1.021)
  Pallas kernels: 59.6 us -> 61.8 us
  local copies, waits for them, and re-layouts: 0.85 us -> 0.01 us
    pallas_call x1, Pallas kernels: 7.91 us -> 9.24 us  [cross(): pl.pallas_call(functools.partial(cross_kernel, rows, owned), out_shape=ja...]
    pallas_call x1, Pallas kernels: 51.7 us -> 52.6 us  [gather(): pl.pallas_call(functools.partial(gather_kernel, rows, cols, groups), out_...]
    unnamed x1 -> x2, local copies, waits for them, and re-layouts: 0.77 us -> 0.01 us
where the time goes in v4:
time: 64 us; the launch traced here: 63.9 us
  Pallas kernels  61.8 us (97%)
  other arithmetic  1.38 us (2%)
  between operations  0.68 us (1%)
    pallas_call x1, Pallas kernels, gather(): pl.pallas_call(functools.partial(gather_kernel, rows, cols, groups), out_...  52.6 us
    pallas_call x1, Pallas kernels, cross(): pl.pallas_call(functools.partial(cross_kernel, rows, owned), out_shape=ja...  9.24 us

profile of v4, /device:TPU:0, one launch (start us, length us, event | category | flops | bytes accessed | tf_op | source)
XLA Modules:
  0.0 63.9 jit_solution(14411948150662951725)
XLA Ops:
  0.7 0.1 pad_add_fusion.place
  0.8 1.3 %multiply_convert_fusion = (bf16[32,1024]{1,0:T(8,128)(2,1)S(1)}, bf16[32,1024]{1,0:T(8,128)(2,1)S(1)}) fusion(f32[1024]{0:T(1024)S(1)} %get-tuple-element.8, s32[32]{0:T(128)} %param.7, f32[1024]{0:T(1024)S(1)} %get-tuple-element.7), kind=kLoop, calls=%fused_computation.6 | loop fusion | flops 589824 | bytes 139392 | tf_op jit(solution)/shard_map/convert_element_type | solution.py:22
  2.0 0.0 copy-start
  2.0 52.6 %shard_map.46.sets = bf16[8,4,32,16,256]{4,3,2,1,0:T(8,128)(2,1)S(1)} custom-call(bf16[16,256,1024]{2,1,0:T(8,128)(2,1)} %rec_hbm.1, bf16[32,1024]{1,0:T(8,128)(2,1)S(1)} %get-tuple-element.6.cos_ref, bf16[32,1024]{1,0:T(8,128)(2,1)S(1)} %get-tuple-element.5.sin_ref), custom_call_target="tpu_custom_call" | custom-call | flops 536870912 | bytes 8388608 | tf_op jit(solution)/shard_map/pallas_call | solution.py:175
  54.6 0.0 copy-done
  54.6 9.2 %shard_map.47 = bf16[1,1,2,2,32,256,256]{6,5,4,3,2,1,0:T(8,128)(2,1)} custom-call(s32[1,1,2,4]{3,2,1,0:T(2,128)S(1)} %bitcast.6, s32[1]{0:T(128)} %bitcast.5.count, s32[3]{0:T(128)S(1)} %pad_add_fusion.place, bf16[8,4,32,16,256]{4,3,2,1,0:T(8,128)(2,1)S(1)} %shard_map.46.sets), custom_call_target="tpu_custom_call" | custom-call | flops 1073741824 | bytes 16777216 | tf_op jit(solution)/shard_map/pallas_call | solution.py:251
  (1 shorter events, 0.0 us)
Async XLA Ops:
  2.0 52.6 %copy-start = (s32[1,1,4,2]{2,3,1,0:T(2,128)S(1)}, s32[1,1,4,2]{2,3,1,0:T(2,128)}, u32[]{:S(2)}) copy-start(s32[1,1,4,2]{2,3,1,0:T(2,128)} %param.5) | copy-start | bytes 100

commit v5 on v4

--- a/solution.py
+++ b/solution.py
@@ -57,7 +57,6 @@
         guarded(way, lambda way=way: pl.semaphore_signal(
             barrier, inc=1, device_id=device[way], device_id_type=pl.DeviceIdType.MESH))
     ends = sum(exists[way].astype(jnp.int32) for way in (UP, DOWN, RIGHT, LEFT))
-    pl.semaphore_wait(barrier, 2 + ends)
 
     def copy(way, src, slot, g):
         return pltpu.make_async_remote_copy(
@@ -103,6 +102,8 @@
         for lane in range(spec.shape[0]):
             own[i, :, :, lane * 128:(lane + 1) * 128] = spec[lane].astype(jnp.bfloat16).reshape(
                 own.shape[1], own.shape[2], 128)
+        if i == 0:
+            pl.semaphore_wait(barrier, 2 + ends)
         for way in (PARTNER, UP, DOWN):
             send(way, own.at[i], r, mine + i)
         for way in (RIGHT, LEFT, SIBLING):
@@ -246,7 +247,7 @@
 
 def cross(sets, pairs, count, place, rows, owned):
     _, groups, bins, entries, channels = sets.shape
-    step = math.gcd(bins, 4)
+    step = math.gcd(bins, 8)
     smem = pl.BlockSpec(memory_space=pltpu.SMEM)
     return pl.pallas_call(
         functools.partial(cross_kernel, rows, owned),

time: 64 us -> 62.5 us (0.977)
  Pallas kernels: 61.8 us -> 60 us
    pallas_call x1, Pallas kernels: 9.24 us -> 7.43 us  [cross(): pl.pallas_call(functools.partial(cross_kernel, rows, owned), out_shape=ja...]
where the time goes in v5:
time: 62.5 us; the launch traced here: 62.1 us
  Pallas kernels  60 us (96%)
  other arithmetic  1.38 us (2%)
  between operations  0.68 us (1%)
    pallas_call x1, Pallas kernels, gather(): pl.pallas_call(functools.partial(gather_kernel, rows, cols, groups), out_...  52.6 us
    pallas_call x1, Pallas kernels, cross(): pl.pallas_call(functools.partial(cross_kernel, rows, owned), out_shape=ja...  7.43 us
    convert_element_type x1, other arithmetic, dft_tables(): return (cosine.astype(jnp.bfloat16), sine.astype(jnp.bfloat16))  1.26 us

profile of v5, /device:TPU:0, one launch (start us, length us, event | category | flops | bytes accessed | tf_op | source)
XLA Modules:
  0.0 62.1 jit_solution(4419384818997106729)
XLA Ops:
  0.7 0.1 pad_add_fusion.place
  0.8 1.3 %multiply_convert_fusion = (bf16[32,1024]{1,0:T(8,128)(2,1)S(1)}, bf16[32,1024]{1,0:T(8,128)(2,1)S(1)}) fusion(f32[1024]{0:T(1024)S(1)} %get-tuple-element.8, s32[32]{0:T(128)} %param.7, f32[1024]{0:T(1024)S(1)} %get-tuple-element.7), kind=kLoop, calls=%fused_computation.6 | loop fusion | flops 589824 | bytes 139392 | tf_op jit(solution)/shard_map/convert_element_type | solution.py:22
  2.0 0.0 copy-start
  2.0 52.6 %shard_map.46.sets = bf16[8,4,32,16,256]{4,3,2,1,0:T(8,128)(2,1)S(1)} custom-call(bf16[16,256,1024]{2,1,0:T(8,128)(2,1)} %rec_hbm.1, bf16[32,1024]{1,0:T(8,128)(2,1)S(1)} %get-tuple-element.6.cos_ref, bf16[32,1024]{1,0:T(8,128)(2,1)S(1)} %get-tuple-element.5.sin_ref), custom_call_target="tpu_custom_call" | custom-call | flops 536870912 | bytes 8388608 | tf_op jit(solution)/shard_map/pallas_call | solution.py:176
  54.6 0.0 copy-done
  54.6 7.4 %shard_map.47 = bf16[1,1,2,2,32,256,256]{6,5,4,3,2,1,0:T(8,128)(2,1)} custom-call(s32[1,1,2,4]{3,2,1,0:T(2,128)S(1)} %bitcast.6, s32[1]{0:T(128)} %bitcast.5.count, s32[3]{0:T(128)S(1)} %pad_add_fusion.place, bf16[8,4,32,16,256]{4,3,2,1,0:T(8,128)(2,1)S(1)} %shard_map.46.sets), custom_call_target="tpu_custom_call" | custom-call | flops 1073741824 | bytes 16777216 | tf_op jit(solution)/shard_map/pallas_call | solution.py:252
  (1 shorter events, 0.0 us)
Async XLA Ops:
  2.0 52.6 %copy-start = (s32[1,1,4,2]{2,3,1,0:T(2,128)S(1)}, s32[1,1,4,2]{2,3,1,0:T(2,128)}, u32[]{:S(2)}) copy-start(s32[1,1,4,2]{2,3,1,0:T(2,128)} %param.5) | copy-start | bytes 100

commit v6 on v5

--- a/solution.py
+++ b/solution.py
@@ -146,9 +146,8 @@
         if h == 1:
             for i in range(groups):
                 along_x(mine + i)
-        if h == max(1, rows - 2):
-            for i in range(groups):
-                along_x(theirs + i)
+    for i in range(groups):
+        along_x(theirs + i)
     extra(r == rows - 2, r == 1)
 
     for h in range(1, rows):

time: 62.5 us -> 62.7 us (level)
  no operation moved by 1% of the time
where the time goes in v6:
time: 62.7 us; the launch traced here: 62.5 us
  Pallas kernels  60.5 us (96%)
  other arithmetic  1.38 us (2%)
  between operations  0.68 us (1%)
    pallas_call x1, Pallas kernels, gather(): pl.pallas_call(functools.partial(gather_kernel, rows, cols, groups), out_...  52.6 us
    pallas_call x1, Pallas kernels, cross(): pl.pallas_call(functools.partial(cross_kernel, rows, owned), out_shape=ja...  7.9 us
    convert_element_type x1, other arithmetic, dft_tables(): return (cosine.astype(jnp.bfloat16), sine.astype(jnp.bfloat16))  1.26 us

profile of v6, /device:TPU:0, one launch (start us, length us, event | category | flops | bytes accessed | tf_op | source)
XLA Modules:
  0.0 62.5 jit_solution(17537295305672069351)
XLA Ops:
  0.7 0.1 pad_add_fusion.place
  0.8 1.3 %multiply_convert_fusion = (bf16[32,1024]{1,0:T(8,128)(2,1)S(1)}, bf16[32,1024]{1,0:T(8,128)(2,1)S(1)}) fusion(f32[1024]{0:T(1024)S(1)} %get-tuple-element.8, s32[32]{0:T(128)} %param.7, f32[1024]{0:T(1024)S(1)} %get-tuple-element.7), kind=kLoop, calls=%fused_computation.6 | loop fusion | flops 589824 | bytes 139392 | tf_op jit(solution)/shard_map/convert_element_type | solution.py:22
  2.0 0.0 copy-start
  2.0 52.6 %shard_map.46.sets = bf16[8,4,32,16,256]{4,3,2,1,0:T(8,128)(2,1)S(1)} custom-call(bf16[16,256,1024]{2,1,0:T(8,128)(2,1)} %rec_hbm.1, bf16[32,1024]{1,0:T(8,128)(2,1)S(1)} %get-tuple-element.6.cos_ref, bf16[32,1024]{1,0:T(8,128)(2,1)S(1)} %get-tuple-element.5.sin_ref), custom_call_target="tpu_custom_call" | custom-call | flops 536870912 | bytes 8388608 | tf_op jit(solution)/shard_map/pallas_call | solution.py:175
  54.6 0.0 copy-done
  54.6 7.9 %shard_map.47 = bf16[1,1,2,2,32,256,256]{6,5,4,3,2,1,0:T(8,128)(2,1)} custom-call(s32[1,1,2,4]{3,2,1,0:T(2,128)S(1)} %bitcast.6, s32[1]{0:T(128)} %bitcast.5.count, s32[3]{0:T(128)S(1)} %pad_add_fusion.place, bf16[8,4,32,16,256]{4,3,2,1,0:T(8,128)(2,1)S(1)} %shard_map.46.sets), custom_call_target="tpu_custom_call" | custom-call | flops 1073741824 | bytes 16777216 | tf_op jit(solution)/shard_map/pallas_call | solution.py:251
  (1 shorter events, 0.0 us)
Async XLA Ops:
  2.0 52.6 %copy-start = (s32[1,1,4,2]{2,3,1,0:T(2,128)S(1)}, s32[1,1,4,2]{2,3,1,0:T(2,128)}, u32[]{:S(2)}) copy-start(s32[1,1,4,2]{2,3,1,0:T(2,128)} %param.5) | copy-start | bytes 100

commit v7 on v5

--- a/solution.py
+++ b/solution.py
@@ -104,7 +104,7 @@
                 own.shape[1], own.shape[2], 128)
         if i == 0:
             pl.semaphore_wait(barrier, 2 + ends)
-        for way in (PARTNER, UP, DOWN):
+        for way in (UP, DOWN, PARTNER):
             send(way, own.at[i], r, mine + i)
         for way in (RIGHT, LEFT, SIBLING):
             send(way, own.at[i], rows + q, mine + i)
@@ -134,15 +134,15 @@
 
     for h in range(1, rows):
         for i in range(groups):
+            shared = () if h == 1 and i == groups - 1 else (PARTNER,)
+            relay(r - h >= 0, r - h, mine + i, (UP,) + shared)
+            relay(r + h < rows, r + h, mine + i, (DOWN,) + shared)
             if h == 1:
                 arrived(r, theirs + i)
                 for way in (RIGHT, LEFT, SIBLING):
                     send(way, sets.at[r, theirs + i], rows + q, theirs + i)
             if h == 1 and i == groups - 1:
                 extra(r < rows - 2, r > 1)
-            shared = () if h == 1 and i == groups - 1 else (PARTNER,)
-            relay(r - h >= 0, r - h, mine + i, (UP,) + shared)
-            relay(r + h < rows, r + h, mine + i, (DOWN,) + shared)
         if h == 1:
             for i in range(groups):
                 along_x(mine + i)

time: 62.5 us -> 60.7 us (0.971)
  Pallas kernels: 60 us -> 58.7 us
    pallas_call x1, Pallas kernels: 52.6 us -> 50.8 us  [gather(): pl.pallas_call(functools.partial(gather_kernel, rows, cols, groups), out_...]
where the time goes in v7:
time: 60.7 us; the launch traced here: 60.8 us
  Pallas kernels  58.7 us (97%)
  other arithmetic  1.38 us (2%)
  between operations  0.68 us (1%)
    pallas_call x1, Pallas kernels, gather(): pl.pallas_call(functools.partial(gather_kernel, rows, cols, groups), out_...  50.8 us
    pallas_call x1, Pallas kernels, cross(): pl.pallas_call(functools.partial(cross_kernel, rows, owned), out_shape=ja...  7.9 us
    convert_element_type x1, other arithmetic, dft_tables(): return (cosine.astype(jnp.bfloat16), sine.astype(jnp.bfloat16))  1.26 us

profile of v7, /device:TPU:0, one launch (start us, length us, event | category | flops | bytes accessed | tf_op | source)
XLA Modules:
  0.0 60.8 jit_solution(2626593812538722781)
XLA Ops:
  0.7 0.1 pad_add_fusion.place
  0.8 1.3 %multiply_convert_fusion = (bf16[32,1024]{1,0:T(8,128)(2,1)S(1)}, bf16[32,1024]{1,0:T(8,128)(2,1)S(1)}) fusion(f32[1024]{0:T(1024)S(1)} %get-tuple-element.8, s32[32]{0:T(128)} %param.7, f32[1024]{0:T(1024)S(1)} %get-tuple-element.7), kind=kLoop, calls=%fused_computation.6 | loop fusion | flops 589824 | bytes 139392 | tf_op jit(solution)/shard_map/convert_element_type | solution.py:22
  2.0 0.0 copy-start
  2.0 50.8 %shard_map.46.sets = bf16[8,4,32,16,256]{4,3,2,1,0:T(8,128)(2,1)S(1)} custom-call(bf16[16,256,1024]{2,1,0:T(8,128)(2,1)} %rec_hbm.1, bf16[32,1024]{1,0:T(8,128)(2,1)S(1)} %get-tuple-element.6.cos_ref, bf16[32,1024]{1,0:T(8,128)(2,1)S(1)} %get-tuple-element.5.sin_ref), custom_call_target="tpu_custom_call" | custom-call | flops 536870912 | bytes 8388608 | tf_op jit(solution)/shard_map/pallas_call | solution.py:176
  52.9 0.0 copy-done
  52.9 7.9 %shard_map.47 = bf16[1,1,2,2,32,256,256]{6,5,4,3,2,1,0:T(8,128)(2,1)} custom-call(s32[1,1,2,4]{3,2,1,0:T(2,128)S(1)} %bitcast.6, s32[1]{0:T(128)} %bitcast.5.count, s32[3]{0:T(128)S(1)} %pad_add_fusion.place, bf16[8,4,32,16,256]{4,3,2,1,0:T(8,128)(2,1)S(1)} %shard_map.46.sets), custom_call_target="tpu_custom_call" | custom-call | flops 1073741824 | bytes 16777216 | tf_op jit(solution)/shard_map/pallas_call | solution.py:252
  (1 shorter events, 0.0 us)
Async XLA Ops:
  2.0 50.8 %copy-start = (s32[1,1,4,2]{2,3,1,0:T(2,128)S(1)}, s32[1,1,4,2]{2,3,1,0:T(2,128)}, u32[]{:S(2)}) copy-start(s32[1,1,4,2]{2,3,1,0:T(2,128)} %param.5) | copy-start | bytes 100

commit v8 on v7

--- a/solution.py
+++ b/solution.py
@@ -143,12 +143,11 @@
                     send(way, sets.at[r, theirs + i], rows + q, theirs + i)
             if h == 1 and i == groups - 1:
                 extra(r < rows - 2, r > 1)
-        if h == 1:
+        if h == max(1, rows - 2):
             for i in range(groups):
                 along_x(mine + i)
-        if h == max(1, rows - 2):
-            for i in range(groups):
-                along_x(theirs + i)
+    for i in range(groups):
+        along_x(theirs + i)
     extra(r == rows - 2, r == 1)
 
     for h in range(1, rows):

time: 60.7 us -> 60.7 us (level)
  no operation moved by 1% of the time
where the time goes in v8:
time: 60.7 us; the launch traced here: 60.8 us
  Pallas kernels  58.7 us (97%)
  other arithmetic  1.38 us (2%)
  between operations  0.68 us (1%)
    pallas_call x1, Pallas kernels, gather(): pl.pallas_call(functools.partial(gather_kernel, rows, cols, groups), out_...  50.8 us
    pallas_call x1, Pallas kernels, cross(): pl.pallas_call(functools.partial(cross_kernel, rows, owned), out_shape=ja...  7.9 us
    convert_element_type x1, other arithmetic, dft_tables(): return (cosine.astype(jnp.bfloat16), sine.astype(jnp.bfloat16))  1.26 us

profile of v8, /device:TPU:0, one launch (start us, length us, event | category | flops | bytes accessed | tf_op | source)
XLA Modules:
  0.0 60.8 jit_solution(2969009434695855038)
XLA Ops:
  0.7 0.1 pad_add_fusion.place
  0.8 1.3 %multiply_convert_fusion = (bf16[32,1024]{1,0:T(8,128)(2,1)S(1)}, bf16[32,1024]{1,0:T(8,128)(2,1)S(1)}) fusion(f32[1024]{0:T(1024)S(1)} %get-tuple-element.8, s32[32]{0:T(128)} %param.7, f32[1024]{0:T(1024)S(1)} %get-tuple-element.7), kind=kLoop, calls=%fused_computation.6 | loop fusion | flops 589824 | bytes 139392 | tf_op jit(solution)/shard_map/convert_element_type | solution.py:22
  2.0 0.0 copy-start
  2.0 50.8 %shard_map.46.sets = bf16[8,4,32,16,256]{4,3,2,1,0:T(8,128)(2,1)S(1)} custom-call(bf16[16,256,1024]{2,1,0:T(8,128)(2,1)} %rec_hbm.1, bf16[32,1024]{1,0:T(8,128)(2,1)S(1)} %get-tuple-element.6.cos_ref, bf16[32,1024]{1,0:T(8,128)(2,1)S(1)} %get-tuple-element.5.sin_ref), custom_call_target="tpu_custom_call" | custom-call | flops 536870912 | bytes 8388608 | tf_op jit(solution)/shard_map/pallas_call | solution.py:175
  52.9 0.0 copy-done
  52.9 7.9 %shard_map.47 = bf16[1,1,2,2,32,256,256]{6,5,4,3,2,1,0:T(8,128)(2,1)} custom-call(s32[1,1,2,4]{3,2,1,0:T(2,128)S(1)} %bitcast.6, s32[1]{0:T(128)} %bitcast.5.count, s32[3]{0:T(128)S(1)} %pad_add_fusion.place, bf16[8,4,32,16,256]{4,3,2,1,0:T(8,128)(2,1)S(1)} %shard_map.46.sets), custom_call_target="tpu_custom_call" | custom-call | flops 1073741824 | bytes 16777216 | tf_op jit(solution)/shard_map/pallas_call | solution.py:251
  (1 shorter events, 0.0 us)
Async XLA Ops:
  2.0 50.8 %copy-start = (s32[1,1,4,2]{2,3,1,0:T(2,128)S(1)}, s32[1,1,4,2]{2,3,1,0:T(2,128)}, u32[]{:S(2)}) copy-start(s32[1,1,4,2]{2,3,1,0:T(2,128)} %param.5) | copy-start | bytes 100
